TPU v7x, 128 devices: a whole 4x4x4 slice. The times are simulated.
128 devices in a mesh: row: 8 (over y_lo, x), col: 16 (over z, y_hi, core).
Axes of the slice: x: 4, y: 4 (y_hi: 2, y_lo: 2; y = y_hi * 2 + y_lo), z: 4, core: 2. Of those that a mesh axis runs over, the one named last changes fastest.
Arguments:
- amplitudes: float32 [16, 3, 1024, 1024], P('row', None, 'col'), may hold values from -6 to 6
- dressing: float32 [1024, 1024], replicated, may hold values from -0.1875 to 0.1875
- integrals: float32 [1024, 3, 16384], P('row', None, 'col'), may hold values from -0.109375 to 0.109375
- occupied_energy: float32 [128], replicated, may hold values from -2 to -0.3
- virtual_energy: float32 [1024], replicated, may hold values from 0.2 to 3
- occupied_rows: int32 [16], P('row'), may hold values from 0 to 127
- virtual_rows: int32 [1024], replicated, may hold values from 0 to 1023
- occupied_columns: int32 [16], P('col'), may hold values from 0 to 127
- virtual_columns: int32 [1024], replicated, may hold values from 0 to 1023
Outputs:
- residual: float32 [16384, 16384], P('row', 'col')
All inputs are finite; a program needn't handle non-finite values.
Results may differ from a plain program's by a relative error of at most 0.00007.
Values sent between devices are 32-bit elements; how exact they have to be, the bound alone decides.
A program may use at most 128 MiB of HBM per device.

v0:
```python
import jax
import jax.numpy as jnp
from jax import lax
from jax.sharding import PartitionSpec as P


def lookup(index, table):
    places = lax.broadcasted_iota(jnp.int32, (index.shape[0], table.shape[0]), 1)
    return jnp.sum(jnp.where(index[:, None] == places, table[None, :], 0.0), axis=1)


def on_device(
    amplitudes,
    dressing,
    integrals,
    occupied_energy,
    virtual_energy,
    occupied_rows,
    virtual_rows,
    occupied_columns,
    virtual_columns,
):
    width = dressing.shape[0]
    dressed = jnp.dot(
        amplitudes.reshape(-1, width), dressing, precision=lax.Precision.HIGHEST
    ).reshape(amplitudes.shape)
    gathered = lax.all_gather(integrals, "row", axis=0, tiled=True)
    rows_here = amplitudes.shape[0]
    virt_count = virtual_rows.shape[0]
    contracted = jnp.einsum(
        "ikac,ckj->iaj",
        lax.all_gather(dressed, "col", axis=2, tiled=True),
        gathered,
        precision=lax.Precision.HIGHEST,
    )
    energy_i = lookup(occupied_rows, occupied_energy)
    energy_a = lookup(virtual_rows, virtual_energy)
    energy_j = lookup(occupied_columns, occupied_energy)
    energy_b = lookup(virtual_columns, virtual_energy)
    denominator = (
        energy_a[None, :, None, None]
        + energy_b[None, None, None, :]
        - energy_i[:, None, None, None]
        - energy_j[None, None, :, None]
    )
    col_count = energy_j.shape[0] * energy_b.shape[0]
    denominator = denominator.reshape(rows_here * virt_count, col_count)
    return contracted.reshape(rows_here * virt_count, col_count) / denominator


def solution(mesh):
    return jax.shard_map(
        on_device,
        mesh=mesh,
        in_specs=(
            P("row", None, "col", None),
            P(),
            P("row", None, "col"),
            P(),
            P(),
            P("row"),
            P(),
            P("col"),
            P(),
        ),
        out_specs=P("row", "col"),
        check_vma=False,
    )
```

profile of v0, /device:TPU:1, one launch (start us, length us, event | category | flops | bytes accessed | tf_op | source)
XLA Modules:
  0.0 394.9 jit_solution(2565075719169129605)
XLA Ops:
  6.5 0.0 copy-start
  6.5 0.0 all-gather.5.cloned.1.call-start
  6.5 0.7 all-gather.5.cloned.1.call-update
  7.3 0.0 copy-start.6
  7.3 0.0 copy-start.7
  7.3 0.0 copy-start.3
  7.3 0.0 copy-start.4
  7.3 0.0 copy-start.5
  7.3 0.0 all-gather.3.cloned.1.call-start
  7.4 0.6 copy-done
  7.9 7.9 %fusion.3 = f32[2,3,64,1024]{3,2,1,0:T(8,128)} fusion(f32[2,3,64,1024]{3,2,1,0:T(8,128)S(1)} %copy-done, f32[1024,1024]{1,0:T(8,128)} %param.10), kind=kOutput, calls=%fused_computation.5 | convolution fusion | flops 4831838208 | bytes 7340032 | tf_op jit(solution)/shard_map/dot_general | solution.py:24
  15.9 0.0 all-gather.3.cloned.1.call-update
  16.5 0.0 copy-done.6
  16.6 0.0 copy-done.7
  16.6 0.2 fusion.5
  16.7 0.1 broadcast_bitcast_fusion
  16.8 0.6 fusion.6
  17.4 0.0 copy-done.3
  17.4 0.0 copy-done.4
  17.4 0.0 copy-done.5
  17.4 1.4 select_reduce_fusion.1
  18.8 2.4 broadcast_add_fusion
  21.2 122.2 %all-gather.5.cloned.1.call-done = f32[1024,3,1024]{2,0,1:T(8,128)} async-done(((f32[128,3,1024]{2,0,1:T(8,128)}), f32[1024,3,1024]{2,0,1:T(8,128)}) %all-gather.5.cloned.1.call-update) | async-done | bytes 12582928 | tf_op jit(solution)/shard_map/all_gather | solution.py:27
  143.4 149.6 %all-gather.3.cloned.1.call-done = f32[2,3,1024,1024]{3,2,1,0:T(8,128)} async-done(((f32[2,3,64,1024]{3,2,1,0:T(8,128)}), f32[2,3,1024,1024]{3,2,1,0:T(8,128)}) %all-gather.3.cloned.1.call-update) | async-done | bytes 25165840 | tf_op jit(solution)/shard_map/all_gather | solution.py:32
  293.0 0.0 copy-start.2
  293.0 88.1 %fusion = f32[2,1024,1024,1]{2,1,3,0:T(8,128)} fusion(f32[2,3,1024,1024]{3,2,1,0:T(8,128)} %all-gather.3.cloned.1.call-done, f32[1024,3,1024]{2,0,1:T(8,128)} %all-gather.5.cloned.1.call-done), kind=kOutput, calls=%fused_computation | convolution fusion | flops 77309411328 | bytes 46137344 | tf_op jit(solution)/shard_map/ikac,ckj->iaj/dot_general | solution.py:30
  381.1 0.0 copy-done.2
  381.1 0.0 copy-start.1
  381.1 6.9 %bitcast_divide_fusion = f32[2048,1024]{1,0:T(8,128)} fusion(f32[2,1024,1024,1]{2,1,3,0:T(8,128)} %fusion, f32[]{:T(128)} %fusion.6, f32[2048]{0:T(1024)S(1)} %bitcast.28, f32[1024,1024]{1,0:T(8,128)S(1)} %copy-done.2), kind=kLoop, calls=%fused_computation.2 | loop fusion | flops 6291456 | bytes 20979716 | tf_op jit(solution)/shard_map/div | solution.py:48
  388.0 0.0 copy-done.1
  (1 shorter events, 0.0 us)
Async XLA Ops:
  6.5 1.4 copy-start
  6.5 136.9 %all-gather.5.cloned.1.call-start = ((), (), s32[]{:S(2)}) async-start(), calls=%async_computation.1 | async-start | bytes 14155776 | tf_op jit(solution)/shard_map/all_gather | solution.py:27
  7.3 9.3 %copy-start.6 = (s32[2]{0:T(128)S(1)}, s32[2]{0:T(128)}, u32[]{:S(2)}) copy-start(s32[2]{0:T(128)} %param.14) | copy-start | bytes 28
  7.3 9.3 %copy-start.7 = (f32[128]{0:T(128)S(1)}, f32[128]{0:T(128)}, u32[]{:S(2)}) copy-start(f32[128]{0:T(128)} %param.12) | copy-start | bytes 1540
  7.3 10.1 %copy-start.3 = (f32[1024]{0:T(1024)S(1)}, f32[1024]{0:T(1024)}, u32[]{:S(2)}) copy-start(f32[1024]{0:T(1024)} %param.13) | copy-start | bytes 12292
  7.3 10.1 %copy-start.4 = (s32[1024]{0:T(1024)S(1)}, s32[1024]{0:T(1024)}, u32[]{:S(2)}) copy-start(s32[1024]{0:T(1024)} %param.15) | copy-start | bytes 12292
  7.3 10.1 %copy-start.5 = (s32[1024]{0:T(1024)S(1)}, s32[1024]{0:T(1024)}, u32[]{:S(2)}) copy-start(s32[1024]{0:T(1024)} %param.17) | copy-start | bytes 12292
  7.3 285.7 %all-gather.3.cloned.1.call-start = ((), (), s32[]{:S(2)}) async-start(), calls=%async_computation | async-start | bytes 26738688 | tf_op jit(solution)/shard_map/all_gather | solution.py:32
  293.0 88.1 %copy-start.2 = (f32[1024,1024]{1,0:T(8,128)S(1)}, f32[1024,1024]{1,0:T(8,128)}, u32[]{:S(2)}) copy-start(f32[1024,1024]{1,0:T(8,128)} %broadcast_add_fusion) | copy-start | bytes 12582916
  381.1 6.9 %copy-start.1 = (f32[2,3,64,1024]{3,2,1,0:T(8,128)S(1)}, f32[2,3,64,1024]{3,2,1,0:T(8,128)}, u32[]{:S(2)}) copy-start(f32[2,3,64,1024]{3,2,1,0:T(8,128)} %param.9) | copy-start | bytes 4718596
Sparse Core Ops, SparseCore 0:
  9.0 134.3 all-gather.4
  145.9 147.0 all-gather.2
where the time goes:
time: 395 us
  waiting for transfers between devices  273 us (69%)
  matrix products  96 us (24%)
  between operations  14.1 us (4%)
  other arithmetic  11.5 us (3%)
    all_gather x1, waiting for transfers between devices, on_device(): lax.all_gather(dressed, 'col', axis=2, tiled=True)  150 us
    all_gather x1, waiting for transfers between devices, on_device(): gathered = lax.all_gather(integrals, 'row', axis=0, tiled=True)  122 us
    dot_general x1, matrix products, on_device(): jnp.einsum('ikac,ckj->iaj', lax.all_gather(dressed, 'col', axis=2, tiled=...  88.1 us
    dot_general x1, matrix products, on_device(): jnp.dot(amplitudes.reshape(-1, width), dressing, precision=lax.Precision....  7.93 us
  transfers between devices with their start and end apart: 2, of which 2 were waited for; matrix products, arithmetic and copies ran while one was open for 3% of the time, Pallas kernels for 0%

commit v1 on v0

v1 whole, which is shorter than its diff:
```python
import functools

import jax
import jax.numpy as jnp
from jax import lax
from jax.experimental import pallas as pl
from jax.experimental.pallas import tpu as pltpu
from jax.sharding import PartitionSpec as P

MESH = pl.DeviceIdType.MESH
BF16, F32 = jnp.bfloat16, jnp.float32
PIECE = 64
BALANCED_W, BALANCED_A = (1,), (1,)


def parts(values):
    high = values.astype(BF16)
    return high, (values - high.astype(F32)).astype(BF16)


def dot(a, b):
    return jnp.dot(a, b, preferred_element_type=F32)


def dot3(a, b_high, b_low):
    a_high, a_low = parts(a)
    return dot(a_high, b_high) + dot(a_high, b_low) + dot(a_low, b_high)


def column(row):
    tiles = [
        jnp.transpose(jnp.broadcast_to(row[:, at : at + 128], (128, 128)))
        for at in range(0, row.shape[1], 128)
    ]
    return jnp.concatenate(tiles, axis=0)


def kernel(
    amp,
    dressing,
    w_in,
    occupied_energy,
    virtual_energy,
    occupied_rows,
    virtual_rows,
    occupied_columns,
    virtual_columns,
    out,
    A,
    W,
    SH,
    SL,
    C,
    EA,
    EB,
    EI,
    send_sem,
    recv_w,
    recv_a,
    local_sem,
    out_sem,
):
    row, col = lax.axis_index("row"), lax.axis_index("col")
    x, ylo = row % 4, row // 4
    z, yhi, core = col // 4, (col // 2) % 2, col % 2

    def source_row(dx, dy):
        return ((ylo + dy) % 2) * 4 + (x + dx) % 4

    def source_col(dz, dy, dcore):
        return ((z + dz) % 4) * 4 + ((yhi + dy) % 2) * 2 + (core + dcore) % 2

    xp, xm, yl = (source_row(1, 0), col), (source_row(3, 0), col), (source_row(0, 1), col)
    zp, zm = (row, source_col(1, 0, 0)), (row, source_col(3, 0, 0))
    yh, sib = (row, source_col(0, 1, 0)), (row, source_col(0, 0, 1))
    neighbours = (xp, xm, yl, zp, zm, yh, sib)

    def rows_w(r, h):
        return pl.ds(pl.multiple_of(r * 128 + h * PIECE, PIECE), PIECE)

    def rows_a(s):
        return pl.ds(pl.multiple_of(s * PIECE, PIECE), PIECE)

    counts = [0, 0, 0]

    def copy_w(k, r, h, target, own=False):
        return pltpu.make_async_remote_copy(
            src_ref=w_in.at[k, pl.ds(h * PIECE, PIECE)] if own else W.at[k, rows_w(r, h)],
            dst_ref=W.at[k, rows_w(r, h)],
            send_sem=send_sem.at[k],
            recv_sem=recv_w.at[k, 2 * r + h],
            device_id=target,
            device_id_type=MESH,
        )

    def copy_a(k, i, s, target):
        return pltpu.make_async_remote_copy(
            src_ref=A.at[k, i, rows_a(s)],
            dst_ref=A.at[k, i, rows_a(s)],
            send_sem=send_sem.at[k],
            recv_sem=recv_a.at[k, i, s],
            device_id=target,
            device_id_type=MESH,
        )

    def send_w(k, r, h, *targets, own=False):
        for target in targets:
            copy_w(k, r, h, target, own).start()
            counts[k] += 1

    def send_a(k, i, s, *targets):
        for target in targets:
            copy_a(k, i, s, target).start()
            counts[k] += 1

    def wait_w(k, r, h):
        copy_w(k, r, h, yl).wait_recv()

    def wait_a(k, i, s):
        copy_a(k, i, s, sib).wait_recv()

    own_w, own_a = source_row(0, 0), source_col(0, 0, 0)

    def start_w(k):
        for first in (0, 1):
            send_w(k, own_w, first, xp, own=True)
            send_w(k, own_w, 1 - first, xm, own=True)
            send_w(k, own_w, first, yl, own=True)

    def start_a(k):
        for first in (0, 1):
            send_a(k, first, own_a, zp)
            send_a(k, 1 - first, own_a, zm)
            send_a(k, first, own_a, yh, sib)

    def pass_first(k, dy):
        on_w = dy == 0 or k not in BALANCED_W
        on_a = dy == 0 or k not in BALANCED_A
        behind, ahead = source_row(3, dy), source_row(1, dy)
        below, above = source_col(3, dy, 0), source_col(1, dy, 0)
        if on_w:
            wait_w(k, behind, 0)
            send_w(k, behind, 0, xp)
            wait_w(k, ahead, 1)
            send_w(k, ahead, 1, xm)
        wait_a(k, 0, below)
        send_a(k, 0, below, *((zp,) if on_a else ()), sib)
        wait_a(k, 1, above)
        send_a(k, 1, above, *((zm,) if on_a else ()), sib)
        wait_a(k, 1, below)
        send_a(k, 1, below, sib)
        wait_a(k, 0, above)
        send_a(k, 0, above, sib)

    def pass_partner(k):
        theirs_w, theirs_a = source_row(0, 1), source_col(0, 1, 0)
        for h in (0, 1):
            wait_w(k, theirs_w, h)
            send_w(k, theirs_w, h, *((xp, xm) if h == 0 else (xm, xp)))
            wait_a(k, h, theirs_a)
            send_a(k, h, theirs_a, *((zp, zm) if h == 0 else (zm, zp)), sib)

    def pass_far(k, dy):
        far_w, far_a = source_row(2, dy), source_col(2, dy, 0)
        for h in (0, 1):
            if dy == 0 and k in BALANCED_W:
                wait_w(k, far_w, h)
                send_w(k, far_w, h, yl)
            wait_a(k, h, far_a)
            send_a(k, h, far_a, *((yh,) if dy == 0 and k in BALANCED_A else ()), sib)

    def rest_w(k, dy):
        on_w = dy == 0 or k not in BALANCED_W
        behind, ahead = source_row(3, dy), source_row(1, dy)
        if not on_w:
            wait_w(k, behind, 0)
            wait_w(k, ahead, 1)
        wait_w(k, behind, 1)
        wait_w(k, ahead, 0)
        if dy == 1 or k not in BALANCED_W:
            for h in (0, 1):
                wait_w(k, source_row(2, dy), h)

    def rest_a(k, dy, steps=(0, 1, 3, 2)):
        for dz in steps:
            for i in (0, 1):
                wait_a(k, i, source_col(dz, dy, 1))

    def split(source, slot, first, count):
        def one(step, _):
            rows = pl.ds(pl.multiple_of(first + step * 64, 64), 64)
            high, low = parts(source[rows])
            SH[slot, rows] = high
            SL[slot, rows] = low
            return 0

        lax.fori_loop(0, count // 64, one, 0)

    def product(k, slot, group, depth_at, depth):
        rows = pl.ds(pl.multiple_of(group * 128, 128), 128)
        if depth == 1024:
            inner = slice(None)
        else:
            inner = pl.ds(pl.multiple_of(depth_at, depth), depth)
        a = A[k, :, rows, inner].reshape(256, depth)
        value = dot3(a, SH[slot, inner], SL[slot, inner])
        return rows, value.reshape(2, 128, 1024)

    def accumulate(k, slot, group, depth_at=0, depth=1024):
        rows, value = product(k, slot, group, depth_at, depth)
        if k == 0:
            C[:, rows] = value
        else:
            C[:, rows] += value

    def out_copy(group):
        rows = pl.ds(pl.multiple_of(group * 128, 128), 128)
        return pltpu.make_async_copy(C.at[:, rows], out.at[:, rows], out_sem.at[group])

    def finish(k, slot, group, depth_at=0, depth=1024):
        rows, value = product(k, slot, group, depth_at, depth)
        sums = jnp.concatenate([EA[rows]] * 8, axis=1) + EB[0:1, :]
        level_j = EI[2:3, 0:1]
        for i in (0, 1):
            denominator = (sums - EI[i : i + 1, 0:1]) - level_j
            C[i, rows] = (C[i, rows] + value[i]) / denominator
        out_copy(group).start()

    def groups(first, last, body):
        def one(group, _):
            body(group)
            return 0

        lax.fori_loop(first, last, one, 0)

    chunk = 256
    loads = [
        pltpu.make_async_copy(
            dressing.at[pl.ds(at, chunk)], C.at[0, pl.ds(at, chunk)], local_sem.at[at // chunk]
        )
        for at in range(0, 1024, chunk)
    ]
    amp_loads = [
        pltpu.make_async_copy(amp.at[:, k], A.at[k, :, rows_a(own_a)], local_sem.at[4 + k])
        for k in range(3)
    ]
    w_load = pltpu.make_async_copy(
        w_in, W.at[:, pl.ds(pl.multiple_of(own_w * 128, 128), 128)], local_sem.at[7]
    )
    for load in (*loads, *amp_loads, w_load):
        load.start()
    barrier = pltpu.get_barrier_semaphore()
    for target in neighbours:
        pl.semaphore_signal(barrier, inc=1, device_id=target, device_id_type=MESH)
    pl.semaphore_wait(barrier, len(neighbours))
    start_w(0)

    for number, load in enumerate(loads):
        load.wait()
        split(C.at[0], 1, number * chunk, chunk)
    for load in amp_loads:
        load.wait()

    def dress(k):
        dressed = dot3(A[k, :, rows_a(own_a)].reshape(128, 1024), SH[1], SL[1])
        A[k, :, rows_a(own_a)] = dressed.reshape(2, PIECE, 1024)

    dress(0)
    start_a(0)
    dress(1)
    dress(2)
    w_load.wait()

    table = virtual_energy[...]
    lanes = lax.broadcasted_iota(jnp.int32, (128, 1024), 1)
    for at in range(0, 1024, 128):
        index = column(virtual_rows[:, at : at + 128])
        index = jnp.concatenate([index] * 8, axis=1)
        found = jnp.sum(jnp.where(index == lanes, table, 0.0), axis=1, keepdims=True)
        EA[at : at + 128] = jnp.broadcast_to(found, (128, 128))
        index = column(virtual_columns[:, at : at + 128])
        index = jnp.concatenate([index] * 8, axis=1)
        found = jnp.sum(jnp.where(index == lanes, table, 0.0), axis=1, keepdims=True)
        found = jnp.transpose(jnp.broadcast_to(found, (128, 128)))
        EB[:, at : at + 128] = found[:8]
    places = lax.broadcasted_iota(jnp.int32, (1, 128), 1)
    levels = (occupied_rows[0], occupied_rows[1], occupied_columns[0])
    for number, place in enumerate(levels):
        level = jnp.sum(
            jnp.where(places == place, occupied_energy[...], 0.0), axis=1, keepdims=True
        )
        EI[number : number + 1] = jnp.broadcast_to(level, (1, 128))

    pass_first(0, 0)
    pass_partner(0)
    start_w(1)
    start_a(1)
    pass_far(0, 0)
    pass_first(0, 1)
    pass_far(0, 1)

    for k in (1, 2):
        for dy in (0, 1):
            rest_w(k - 1, dy)
            rest_a(k - 1, dy)
        slot = (k - 1) % 2
        split(W.at[k - 1], slot, 0, 1024)
        groups(0, 4, functools.partial(accumulate, k - 1, slot))
        pass_first(k, 0)
        groups(4, 8, functools.partial(accumulate, k - 1, slot))
        pass_partner(k)
        if k == 1:
            start_w(2)
            start_a(2)
            pass_far(k, 0)
            pass_first(k, 1)
            pass_far(k, 1)
    pass_far(2, 0)

    ours, theirs = ylo * 512, (1 - ylo) * 512
    rest_w(2, 0)
    rest_a(2, 0)
    split(W.at[2], 0, ours, 512)
    groups(0, 4, lambda n: accumulate(2, 0, 2 * n + yhi, ours, 512))
    pass_first(2, 1)
    rest_a(2, 1, (0, 1, 3))
    other = 1 - yhi
    for dz in (0, 1, 3):
        accumulate(2, 0, ((z + dz) % 4) * 2 + other, ours, 512)
    pass_far(2, 1)
    rest_w(2, 1)
    split(W.at[2], 0, theirs, 512)
    groups(0, 4, lambda n: finish(2, 0, 2 * n + yhi, theirs, 512))
    for dz in (0, 1, 3):
        finish(2, 0, ((z + dz) % 4) * 2 + other, theirs, 512)
    rest_a(2, 1, (2,))
    finish(2, 0, ((z + 2) % 4) * 2 + other)

    for k in range(3):
        share = A.at[0:2, :, pl.ds(0, counts[k] * PIECE // 4)]
        pltpu.make_async_remote_copy(
            src_ref=share,
            dst_ref=share,
            send_sem=send_sem.at[k],
            recv_sem=recv_a.at[0, 0, 0],
            device_id=sib,
            device_id_type=MESH,
        ).wait_send()
    for group in range(8):
        out_copy(group).wait()


def on_device(
    amplitudes,
    dressing,
    integrals,
    occupied_energy,
    virtual_energy,
    occupied_rows,
    virtual_rows,
    occupied_columns,
    virtual_columns,
):
    anywhere = pl.BlockSpec(memory_space=pl.ANY)
    vmem = pl.BlockSpec(memory_space=pltpu.VMEM)
    smem = pl.BlockSpec(memory_space=pltpu.SMEM)
    residual = pl.pallas_call(
        kernel,
        out_shape=jax.ShapeDtypeStruct((2, 1024, 1024), F32),
        in_specs=[anywhere, anywhere, anywhere, vmem, vmem, smem, vmem, smem, vmem],
        out_specs=anywhere,
        scratch_shapes=[
            pltpu.VMEM((3, 2, 1024, 1024), F32),
            pltpu.VMEM((3, 1024, 1024), F32),
            pltpu.VMEM((2, 1024, 1024), BF16),
            pltpu.VMEM((2, 1024, 1024), BF16),
            pltpu.VMEM((2, 1024, 1024), F32),
            pltpu.VMEM((1024, 128), F32),
            pltpu.VMEM((8, 1024), F32),
            pltpu.VMEM((8, 128), F32),
            pltpu.SemaphoreType.DMA((3,)),
            pltpu.SemaphoreType.DMA((3, 16)),
            pltpu.SemaphoreType.DMA((3, 2, 16)),
            pltpu.SemaphoreType.DMA((8,)),
            pltpu.SemaphoreType.DMA((8,)),
        ],
        compiler_params=pltpu.CompilerParams(
            collective_id=0, has_side_effects=True, vmem_limit_bytes=58 * 2**20
        ),
        cost_estimate=pl.CostEstimate(
            flops=42_000_000_000, bytes_accessed=20_000_000, transcendentals=0
        ),
    )(
        amplitudes,
        dressing,
        jnp.transpose(integrals, (1, 0, 2)),
        occupied_energy.reshape(1, -1),
        virtual_energy.reshape(1, -1),
        occupied_rows,
        virtual_rows.reshape(1, -1),
        occupied_columns,
        virtual_columns.reshape(1, -1),
    )
    return residual.reshape(2048, 1024)


def solution(mesh):
    return jax.shard_map(
        on_device,
        mesh=mesh,
        in_specs=(
            P("row", None, "col", None),
            P(),
            P("row", None, "col"),
            P(),
            P(),
            P("row"),
            P(),
            P("col"),
            P(),
        ),
        out_specs=P("row", "col"),
        check_vma=False,
    )
```

time: 395 us -> 177 us (0.45)
  waiting for transfers between devices: 273 us -> 0 us
  Pallas kernels: 0 us -> 167 us
  matrix products: 96 us -> 0 us
  between operations: 14.1 us -> 0.66 us
  other arithmetic: 11.5 us -> 0 us
  local copies, waits for them, and re-layouts: 0.7 us -> 8.44 us
    all_gather x2 -> x0, waiting for transfers between devices: 272 us -> none  [the longest x1 150 us: on_device(): lax.all_gather(dressed, 'col', axis=2, tiled=True)]
    pallas_call x0 -> x1, Pallas kernels: none -> 167 us  [on_device(): pl.pallas_call(kernel, out_shape=jax.ShapeDtypeStruct((2, 1024, 1024), F3...]
    dot_general x2 -> x0, matrix products: 96 us -> none  [the longest x1 88.1 us: on_device(): jnp.einsum('ikac,ckj->iaj', lax.all_gather(dressed, 'col', axis=2, tiled=...]
    unnamed x18 -> x1, local copies, waits for them, and re-layouts: 0.7 us -> 8.44 us
    div x1 -> x0, other arithmetic: 6.94 us -> none  [on_device(): return contracted.reshape(rows_here * virt_count, col_count) / denominator]
  transfers between devices with their start and end apart: 2 -> 0, of which waited for: 2 -> 0; matrix products, arithmetic and copies ran while one was open for 3% -> 0% of each run, Pallas kernels for 0% -> 0%
where the time goes in v1:
time: 177 us; the launch traced here: 176 us
  Pallas kernels  167 us (94%)
  local copies, waits for them, and re-layouts  8.44 us (5%)
    pallas_call x1, Pallas kernels, on_device(): pl.pallas_call(kernel, out_shape=jax.ShapeDtypeStruct((2, 1024, 1024), F3...  167 us
    unnamed x1, local copies, waits for them, and re-layouts  8.44 us

profile of v1, /device:TPU:1, one launch (start us, length us, event | category | flops | bytes accessed | tf_op | source)
XLA Modules:
  0.0 176.0 jit_solution(16738126703403618200)
XLA Ops:
  0.7 166.9 %shard_map.91 = f32[2,1024,1024]{2,1,0:T(8,128)} custom-call(f32[2,3,64,1024]{3,2,1,0:T(8,128)} %amp.1, f32[1024,1024]{1,0:T(8,128)} %dressing.1, f32[3,128,1024]{2,1,0:T(8,128)} %bitcast.7, f32[1,128]{1,0:T(1,128)} %bitcast.11, f32[1,1024]{1,0:T(1,128)} %bitcast.8, s32[2]{0:T(128)} %occupied_rows.1, s32[1,1024]{1,0:T(1,128)} %bitcast.9, ...), custom_call_target="tpu_custom_call" | custom-call | flops 41999998976 | bytes 20000000 | tf_op jit(solution)/shard_map/pallas_call | solution.py:367
  167.6 8.4 %copy.12 = f32[2048,1024]{1,0:T(8,128)} copy(f32[2048,1024]{1,0:T(8,128)} %bitcast.6) | data formatting | bytes 16777216
